TPU v7x, 512 devices: a whole 4x4x16 slice. The times are simulated.
512 devices in a mesh: rows: 32 (over z, core), pairs: 16 (over y, x).
Axes of the slice: x: 4, y: 4, z: 16, core: 2. Of those that a mesh axis runs over, the one named last changes fastest.
Arguments:
- matrix: float32 [4096, 8192], P('rows', 'pairs'), may hold values from -40 to 40
- plan: int32 [2, 64], replicated, may hold values from 0 to 63, as said below
Outputs:
- rotated_matrix: float32 [4096, 8192], P('rows', 'pairs')
Inputs may be any that keep to these rules, and one draw needn't show every extreme that they name: Each row plan[r] is a permutation of the 64 slots. Slots 4 j .. 4 j + 3 are those of index j of pairs. From one arrangement to the next at most one block goes from each index j to j + 1 and at most one to j - 1 (none farther and none from the last index to the first or back); all other blocks stay at their index.
All inputs are finite; a program needn't handle non-finite values.
Results may differ from a plain program's by a relative error of at most 0.0003.
Values sent between devices are 32-bit elements; how exact they have to be, the bound alone decides.
A program may use at most 128 MiB of HBM per device.

v0:
```python
import jax
import jax.numpy as jnp
import numpy as np
from jax import lax
from jax.sharding import PartitionSpec as P

BLK = 128
ROUNDS = 2
STEPS = 4


def from_behind(block, axis, distance):
    devices = range(lax.axis_size(axis))
    route = [(i - distance, i) for i in devices if i - distance in devices]
    return lax.ppermute(block, axis, route)


def tournament(full_width, steps_count):
    half_cols = full_width // 2

    def place(position):
        return position if position < half_cols else full_width - 1 - position + half_cols

    def before(position):
        if position == 0:
            return 0
        if position == 1:
            return full_width - 1
        return position - 1

    start = np.zeros(full_width, dtype=np.int32)
    moves = np.zeros(full_width, dtype=np.int32)
    for position in range(full_width):
        start[place(position)] = position
        moves[place(position)] = place(before(position))
    layout = start.copy()
    for step_no in range(steps_count):
        layout = layout[moves]
    undo = np.argsort(layout).astype(np.int32)
    return (start, moves, undo)


def take_static(array_in, index_list, axis_no):
    pieces = []
    first = 0
    total = len(index_list)
    while first < total:
        last = first
        while last + 1 < total and int(index_list[last + 1]) == int(index_list[last]) + 1:
            last = last + 1
        begin = int(index_list[first])
        pieces.append(lax.slice_in_dim(array_in, begin, begin + last - first + 1, axis=axis_no))
        first = last + 1
    if len(pieces) == 1:
        return pieces[0]
    return jnp.concatenate(pieces, axis=axis_no)


def jacobi_tangent(upper_a, lower_b, coupling):
    differ = lower_b - upper_a
    sign_val = jnp.where(differ >= 0.0, 1.0, -1.0)
    denom = jnp.abs(differ) + jnp.sqrt(differ * differ + 4.0 * coupling * coupling)
    positive = denom > 0.0
    safe_den = jnp.where(positive, denom, 1.0)
    return jnp.where(positive, 2.0 * coupling * sign_val / safe_den, 0.0)


def rotate_gram(gram_mat, steps_count):
    full_width = gram_mat.shape[-1]
    half_cols = full_width // 2
    start, moves, undo = tournament(full_width, steps_count)
    current = take_static(take_static(gram_mat, start, 1), start, 2)
    vectors = jnp.broadcast_to(
        jnp.asarray(np.eye(full_width, dtype=np.float32)[:, start]), gram_mat.shape
    )
    for step_no in range(steps_count):
        upper_a = jnp.diagonal(current[:, :half_cols, :half_cols], axis1=1, axis2=2)
        lower_b = jnp.diagonal(current[:, half_cols:, half_cols:], axis1=1, axis2=2)
        coupling = jnp.diagonal(current[:, :half_cols, half_cols:], axis1=1, axis2=2)
        tangent = jacobi_tangent(upper_a, lower_b, coupling)
        cosine = 1.0 / jnp.sqrt(1.0 + tangent * tangent)
        sine_val = cosine * tangent
        col_cos = cosine[:, None, :]
        col_sin = sine_val[:, None, :]
        left_part = current[:, :, :half_cols]
        right_part = current[:, :, half_cols:]
        current = jnp.concatenate(
            [
                left_part * col_cos - right_part * col_sin,
                left_part * col_sin + right_part * col_cos,
            ],
            axis=2,
        )
        row_cos = cosine[:, :, None]
        row_sin = sine_val[:, :, None]
        top_part = current[:, :half_cols, :]
        bottom_part = current[:, half_cols:, :]
        current = jnp.concatenate(
            [
                top_part * row_cos - bottom_part * row_sin,
                top_part * row_sin + bottom_part * row_cos,
            ],
            axis=1,
        )
        left_vec = vectors[:, :, :half_cols]
        right_vec = vectors[:, :, half_cols:]
        vectors = jnp.concatenate(
            [left_vec * col_cos - right_vec * col_sin, left_vec * col_sin + right_vec * col_cos],
            axis=2,
        )
        current = take_static(take_static(current, moves, 1), moves, 2)
        vectors = take_static(vectors, moves, 2)
    return take_static(vectors, undo, 2)


def on_device(matrix, plan):
    local_rows = matrix.shape[0]
    slot_count = matrix.shape[1] // BLK
    device_no = lax.axis_index("pairs")
    first_slot = device_no * slot_count
    blocks = matrix.reshape(local_rows, slot_count, BLK)
    for round_no in range(ROUNDS):
        sources = plan[round_no].reshape(-1, slot_count)
        padded = jnp.pad(sources, ((1, 1), (0, 0)), constant_values=-1)
        mine = lax.dynamic_index_in_dim(padded, device_no + 1, 0, keepdims=False)
        from_left = from_behind(blocks, "pairs", 1)
        from_right = from_behind(blocks, "pairs", -1)
        offsets = jnp.arange(3 * slot_count, dtype=jnp.int32) + first_slot - slot_count
        candidates = jnp.concatenate([from_left, blocks, from_right], axis=1)
        picker = (mine[:, None] == offsets[None, :]).astype(jnp.float32)
        arranged = jnp.einsum("rkc,sk->rsc", candidates, picker, precision=lax.Precision.HIGHEST)
        paired = arranged.reshape(local_rows, slot_count // 2, 2 * BLK)
        local_gram = jnp.einsum("rpi,rpj->pij", paired, paired, precision=lax.Precision.HIGHEST)
        gram_mat = lax.psum(local_gram, "rows")
        rotation = rotate_gram(gram_mat, STEPS)
        paired = jnp.einsum("rpi,pij->rpj", paired, rotation, precision=lax.Precision.HIGHEST)
        blocks = paired.reshape(local_rows, slot_count, BLK)
    return blocks.reshape(local_rows, slot_count * BLK)


def solution(mesh):
    return jax.shard_map(
        on_device,
        mesh=mesh,
        in_specs=(P("rows", "pairs"), P()),
        out_specs=P("rows", "pairs"),
        check_vma=False,
    )
```

profile of v0, /device:TPU:1, one launch (start us, length us, event | category | flops | bytes accessed | tf_op | source)
XLA Modules:
  0.0 864.4 jit_solution(17649573790734282468)
XLA Ops:
  8.9 4.6 collective-permute-start
  19.1 218.6 %all-reduce.5.cloned.1.call-done = f32[2,256,256]{2,1,0:T(8,128)} async-done(((f32[2,256,256]{2,1,0:T(8,128)}), f32[2,256,256]{2,1,0:T(8,128)}) %all-reduce.5.cloned.1.call-update) | async-done | bytes 524304 | tf_op jit(solution)/shard_map/psum | solution.py:134
  249.3 2.0 fusion.128
  251.3 3.6 fusion.123
  254.9 3.5 fusion.124
  258.5 3.5 fusion.126
  262.0 3.6 fusion.127
  265.5 3.5 fusion.122
  269.0 3.5 fusion.125
  272.6 24.3 %concatenate.201 = f32[2,256,128]{2,1,0:T(8,128)S(1)} concatenate(f32[2,256,1]{2,1,0:T(8,128)} %get-tuple-element.471, f32[2,256,1]{2,1,0:T(8,128)} %get-tuple-element.470, f32[2,256,1]{2,1,0:T(8,128)} %get-tuple-element.469, f32[2,256,1]{2,1,0:T(8,128)} %get-tuple-element.468, f32[2,256,1]{2,1,0:T(8,128)} %get-tuple-element.467, f32[2,256,1]{2,1,0:T(8,128)S(1)} %get-tuple-element.466, ...), dimensions={2} | concatenate | bytes 524288 | tf_op jit(solution)/shard_map/concatenate | solution.py:56
  296.9 4.7 copy.135
  301.7 1.8 gather_fusion
  304.5 4.7 copy.136
  311.1 4.7 copy.139
  320.2 4.7 copy.141
  326.8 4.7 copy.142
  333.4 4.7 copy.145
  342.2 4.7 copy.147
  348.8 4.7 copy.148
  355.4 5.1 copy.151
  360.5 1.8 gather_fusion.8
  364.4 4.7 copy.153
  371.2 4.7 copy.154
  377.8 4.7 copy.157
  385.7 2.0 fusion.156
  387.7 3.6 fusion.151
  391.4 3.5 fusion.154
  394.9 3.6 fusion.152
  398.5 3.5 fusion.153
  402.0 3.5 fusion.150
  405.5 3.5 fusion.155
  409.9 24.8 %concatenate.222 = f32[2,256,256]{2,1,0:T(8,128)S(1)} concatenate(f32[2,256,1]{2,1,0:T(8,128)S(1)} %bitcast.200, f32[2,256,124]{2,1,0:T(8,128)} %slice.4359, f32[2,256,1]{2,1,0:T(8,128)} %get-tuple-element.872, f32[2,256,1]{2,1,0:T(8,128)} %get-tuple-element.871, f32[2,256,1]{2,1,0:T(8,128)} %get-tuple-element.870, f32[2,256,1]{2,1,0:T(8,128)} %get-tuple-element.869, ...), dimensions={2} | concatenate | bytes 1048576 | tf_op jit(solution)/shard_map/concatenate | solution.py:56
  437.1 4.2 collective-permute-start.2
  441.4 3.8 collective-permute-done.3
  448.4 210.7 %all-reduce.7.cloned.1.call-done = f32[2,256,256]{2,1,0:T(8,128)} async-done(((f32[2,256,256]{2,1,0:T(8,128)}), f32[2,256,256]{2,1,0:T(8,128)}) %all-reduce.7.cloned.1.call-update) | async-done | bytes 524304 | tf_op jit(solution)/shard_map/psum | solution.py:134
  670.7 2.0 fusion.111
  672.7 3.6 fusion.106
  676.3 3.5 fusion.107
  679.9 3.5 fusion.109
  683.4 3.6 fusion.110
  687.0 3.5 fusion.105
  690.4 3.5 fusion.108
  694.0 24.3 %concatenate.225 = f32[2,256,128]{2,1,0:T(8,128)S(1)} concatenate(f32[2,256,1]{2,1,0:T(8,128)} %get-tuple-element.201, f32[2,256,1]{2,1,0:T(8,128)} %get-tuple-element.200, f32[2,256,1]{2,1,0:T(8,128)} %get-tuple-element.199, f32[2,256,1]{2,1,0:T(8,128)} %get-tuple-element.198, f32[2,256,1]{2,1,0:T(8,128)} %get-tuple-element.197, f32[2,256,1]{2,1,0:T(8,128)S(1)} %get-tuple-element.196, ...), dimensions={2} | concatenate | bytes 524288 | tf_op jit(solution)/shard_map/concatenate | solution.py:56
  718.4 4.7 copy.166
  725.9 4.7 copy.167
  732.5 4.7 copy.170
  741.0 4.7 copy.172
  747.6 4.7 copy.173
  754.2 4.7 copy.176
  763.0 4.7 copy.178
  769.6 4.7 copy.179
  776.2 5.0 copy.182
  781.2 1.8 gather_fusion.20
  785.1 4.7 copy.184
  791.8 4.7 copy.185
  798.4 4.7 copy.188
  806.3 2.0 fusion.142
  808.3 3.6 fusion.137
  812.0 3.5 fusion.140
  815.5 3.6 fusion.138
  819.1 3.5 fusion.139
  822.6 3.5 fusion.136
  826.1 3.5 fusion.141
  830.5 24.8 %concatenate.245 = f32[2,256,256]{2,1,0:T(8,128)S(1)} concatenate(f32[2,256,1]{2,1,0:T(8,128)S(1)} %bitcast.201, f32[2,256,124]{2,1,0:T(8,128)} %slice.4814, f32[2,256,1]{2,1,0:T(8,128)} %get-tuple-element.730, f32[2,256,1]{2,1,0:T(8,128)} %get-tuple-element.729, f32[2,256,1]{2,1,0:T(8,128)} %get-tuple-element.728, f32[2,256,1]{2,1,0:T(8,128)} %get-tuple-element.727, ...), dimensions={2} | concatenate | bytes 1048576 | tf_op jit(solution)/shard_map/concatenate | solution.py:56
  (221 shorter events, 96.7 us)
Async XLA Ops:
  6.5 231.2 %all-reduce.5.cloned.1.call-start = ((), (), s32[]{:S(2)}) async-start(), calls=%async_computation | async-start | bytes 1048576 | tf_op jit(solution)/shard_map/psum | solution.py:134
  7.6 7.7 collective-permute-start.1
  8.9 7.9 collective-permute-start
  19.1 640.1 %all-reduce.7.cloned.1.call-start = ((), (), s32[]{:S(2)}) async-start(), calls=%async_computation.1 | async-start | bytes 1048576 | tf_op jit(solution)/shard_map/psum | solution.py:134
  304.5 13.2 %copy-start.1 = (f32[256,128]{1,0:T(8,128)S(1)}, f32[256,128]{1,0:T(8,128)}, u32[]{:S(2)}) copy-start(f32[256,128]{1,0:T(8,128)} %constant.93) | copy-start | bytes 393220
  304.5 13.2 %copy-start.2 = (f32[256,128]{1,0:T(8,128)S(1)}, f32[256,128]{1,0:T(8,128)}, u32[]{:S(2)}) copy-start(f32[256,128]{1,0:T(8,128)} %constant.92) | copy-start | bytes 393220
  326.8 13.2 %copy-start = (f32[2,256,126]{2,1,0:T(8,128)S(1)}, f32[2,256,126]{2,1,0:T(8,128)}, u32[]{:S(2)}) copy-start(f32[2,256,126]{2,1,0:T(8,128)} %slice.4296) | copy-start | bytes 774148
  435.8 9.4 %collective-permute-start.3 = (f32[128,4,128]{2,1,0:T(4,128)S(1)}, f32[128,4,128]{2,1,0:T(4,128)S(1)}, u32[]{:S(2)}, u32[]{:S(2)}) collective-permute-start(f32[128,4,128]{2,1,0:T(4,128)S(1)} %copy.161), channel_id=1, source_target_pairs={{1,0},{2,1},{3,2},{4,3},{5,4},{6,5},{7,6},{8,7},{9,8},{10,9},{11,1... | collective-permute-start | bytes 786440 | tf_op jit(solution)/shard_map/ppermute | solution.py:15
  437.1 9.0 %collective-permute-start.2 = (f32[128,4,128]{2,1,0:T(4,128)S(1)}, f32[128,4,128]{2,1,0:T(4,128)S(1)}, u32[]{:S(2)}, u32[]{:S(2)}) collective-permute-start(f32[128,4,128]{2,1,0:T(4,128)S(1)} %copy.161), channel_id=1, source_target_pairs={{0,1},{1,2},{2,3},{3,4},{4,5},{5,6},{6,7},{7,8},{8,9},{9,10},{10,1... | collective-permute-start | bytes 786440 | tf_op jit(solution)/shard_map/ppermute | solution.py:15
  725.9 13.2 %copy-start.3 = (f32[256,128]{1,0:T(8,128)S(1)}, f32[256,128]{1,0:T(8,128)}, u32[]{:S(2)}) copy-start(f32[256,128]{1,0:T(8,128)} %constant.92) | copy-start | bytes 393220
Sparse Core Ops, SparseCore 0:
  19.2 218.4 all-reduce.4
  448.6 210.5 all-reduce.6
where the time goes:
time: 880 us; the launch traced here: 864 us
  waiting for transfers between devices  436 us (50%)
  local copies, waits for them, and re-layouts  388 us (44%)
  between operations  15 us (2%)
  starting transfers between devices  11.4 us (1%)
    psum x2, waiting for transfers between devices, on_device(): gram_mat = lax.psum(local_gram, 'rows')  429 us
    slice x109, local copies, waits for them, and re-layouts, take_static(): lax.slice_in_dim(array_in, begin, begin + last - first + 1, axis=axis_no)  123 us
    concatenate x12, local copies, waits for them, and re-layouts, take_static(): return jnp.concatenate(pieces, axis=axis_no)  101 us
    slice x14, local copies, waits for them, and re-layouts, rotate_gram(): upper_a = jnp.diagonal(current[:, :half_cols, :half_cols], axis1=1, axis2=2)  39.8 us
    slice x8, local copies, waits for them, and re-layouts, rotate_gram(): current[:, :half_cols, half_cols:]  38.5 us
    slice x10, local copies, waits for them, and re-layouts, rotate_gram(): lower_b = jnp.diagonal(current[:, half_cols:, half_cols:], axis1=1, axis2=2)  37.9 us
  transfers between devices with their start and end apart: 6, of which 6 were waited for; matrix products, arithmetic and copies ran while one was open for 0% of the time, Pallas kernels for 0%

commit v1 on v0

v1 whole, which is shorter than its diff:
```python
import functools

import jax
import jax.numpy as jnp
from jax import lax
from jax.experimental import pallas as pl
from jax.experimental.pallas import tpu as pltpu
from jax.sharding import PartitionSpec as P

MESH = pl.DeviceIdType.MESH
BLK = 128
ROUNDS = 2
STEPS = 4
SLOTS = 4
GROUP = 4
LANES = 128
F32 = jnp.float32
HOPS = ((2, 0), (2, 1), (3, 0), (3, 1), (1, 0), (1, 1), (0, 1))


def roll(x, by):
    return pltpu.roll(x, by % x.shape[1], 1)


def lane_of(shape):
    return lax.broadcasted_iota(jnp.int32, shape, 1)


def pick(x, index):
    return jnp.take_along_axis(x, index, axis=1)


def extra_lanes(slot):
    first = jnp.where(slot < 3, 0, jnp.where(slot < 5, 1, 2))
    second = jnp.where(slot < 3, 2 * slot + 1, jnp.where(slot == 3, 2, jnp.where(slot == 4, 4, 3)))
    return first, jnp.minimum(second, 7)


def band_terms(left, right, reverse):
    lane = lane_of(left.shape)
    top, bottom = left, pick(right, reverse)
    back = pick(left, reverse)
    tops = [top] + [roll(jnp.where(lane < d, right, top), -d) for d in (2, 4, 6)]
    bottoms = [bottom] + [roll(jnp.where(lane < d, back, bottom), -d) for d in (2, 4, 6)]
    first, second = extra_lanes(lane % 8)
    one = jnp.where(lane < 16, pick(top, first), pick(bottom, first))
    two = jnp.where(lane % 16 < 8, pick(top, second), pick(bottom, second))
    terms = [top * t for t in tops] + [top * b for b in bottoms]
    terms += [one * two] + [bottom * t for t in tops[1:]] + [bottom * b for b in bottoms]
    return top, bottom, terms


def tangent_of(upper_a, lower_b, coupling):
    differ = lower_b - upper_a
    sign_val = jnp.where(differ >= 0.0, 1.0, -1.0)
    denom = jnp.abs(differ) + jnp.sqrt(differ * differ + 4.0 * coupling * coupling)
    positive = denom > 0.0
    safe_den = jnp.where(positive, denom, 1.0)
    return jnp.where(positive, 2.0 * coupling * sign_val / safe_den, 0.0)


def rotate_both(top, bottom, cosine, sine):
    return top * cosine - bottom * sine, top * sine + bottom * cosine


def angles(tt, tb, bt, bb):
    shape = tt.shape
    lane = lane_of(shape)
    row = lax.broadcasted_iota(jnp.int32, shape, 0)
    first, second = extra_lanes(jnp.minimum(lane, 5))
    ahead = lane + 2 * row
    over = ahead > LANES - 1
    is_extra = row == 4
    at_i = jnp.where(is_extra, first, lane)
    at_j = jnp.where(is_extra, second, jnp.where(row > 4, lane, jnp.where(over, 2 * LANES - 1 - ahead, ahead)))
    flip = jnp.where(over & (row < 4), -1.0, 1.0)

    def line(x, r):
        return jnp.broadcast_to(x[r : r + 1], shape)

    def item(x, r, i):
        return jnp.broadcast_to(x[r : r + 1, i : i + 1], shape)

    def up(x):
        return pltpu.roll(x, shape[0] - 1, 0)

    def down(x):
        return pltpu.roll(x, 1, 0)

    cosines, sines = [], []
    for step_no in range(STEPS):
        tangent = tangent_of(line(tt, 0), line(bb, 0), line(tb, 0))
        cosine = 1.0 / jnp.sqrt(1.0 + tangent * tangent)
        sine = cosine * tangent
        cosines.append(cosine[0:1])
        sines.append(sine[0:1])
        if step_no == STEPS - 1:
            break
        cos_i, sin_i = pick(cosine, at_i), pick(sine, at_i)
        cos_j, sin_j = pick(cosine, at_j), pick(sine, at_j) * flip
        tt, tb = rotate_both(tt, tb, cos_j, sin_j)
        bt, bb = rotate_both(bt, bb, cos_j, sin_j)
        tt, bt = rotate_both(tt, bt, cos_i, sin_i)
        tb, bb = rotate_both(tb, bb, cos_i, sin_i)
        new_tt = jnp.where(
            lane >= 2,
            roll(tt, 1),
            jnp.where(
                lane == 1,
                jnp.where(row == 0, roll(bb, 1), roll(bt, 1)),
                jnp.where(row == 0, tt, pick(line(tt, 4), jnp.maximum(row - 1, 0))),
            ),
        )
        new_bb = jnp.where(lane < LANES - 1, roll(bb, -1), pick(tt, LANES - 1 - 2 * row))
        new_tb = jnp.where(
            lane >= 2,
            roll(up(tb), 1),
            jnp.where(lane == 1, roll(up(bb), 1), pick(line(tb, 4), row)),
        )
        new_bt = jnp.where(
            row == 0,
            new_tb,
            jnp.where(
                lane < LANES - 1,
                roll(down(bt), -1),
                pick(down(bt), jnp.minimum(LANES + 1 - 2 * row, LANES - 1)),
            ),
        )
        head = lane == 0
        second_one = lane == 1
        extra_tt = jnp.where(head, item(tb, 0, 0), jnp.where(second_one, item(tt, 1, 0), item(bt, 4, 0)))
        extra_tb = jnp.where(head, item(tb, 1, 0), jnp.where(second_one, item(tb, 2, 0), item(bb, 4, 1)))
        extra_bt = jnp.where(head, item(bb, 4, 0), jnp.where(second_one, item(bt, 4, 3), item(tb, 4, 3)))
        extra_bb = jnp.where(head, item(bb, 4, 3), jnp.where(second_one, item(bb, 4, 4), item(bb, 4, 5)))
        tt = jnp.where(is_extra, extra_tt, new_tt)
        tb = jnp.where(is_extra, extra_tb, new_tb)
        bt = jnp.where(is_extra, extra_bt, new_bt)
        bb = jnp.where(is_extra, extra_bb, new_bb)
    return cosines, sines


def apply_steps(top, bottom, cosines, sines):
    lane = lane_of(top.shape)
    for step_no in range(STEPS):
        top, bottom = rotate_both(top, bottom, cosines[step_no], sines[step_no])
        if step_no < STEPS - 1:
            new_top = jnp.where(lane == 0, top, roll(jnp.where(lane == 0, bottom, top), 1))
            bottom = jnp.where(lane == LANES - 1, top, roll(bottom, -1))
            top = new_top
    last = STEPS - 1
    turn = 2 * LANES - 1 - last
    keep = LANES - last
    left = jnp.where(
        lane == 0,
        top,
        jnp.where(lane < keep, roll(top, -last), pick(bottom, jnp.minimum(turn - lane, LANES - 1))),
    )
    right = jnp.where(
        lane < keep, pick(bottom, jnp.maximum(turn - LANES - lane, 0)), roll(top, LANES - 1 - last)
    )
    return left, right


def kernel(
    n_rows, n_pairs, plan_ref, x_ref, o_ref,
    first, second, came, sent, sides, result, bands, parts, sums, entries, turns,
    in_sem, out_sem, block_out, block_in, part_out, part_in, sum_out, sum_in, turn_out, turn_in,
):
    rows_at = lax.axis_index("rows")
    index = lax.axis_index("pairs")
    z, core = rows_at // 2, rows_at % 2
    n_chips = n_rows // 2
    group, member = z // GROUP, z % GROUP
    local_rows = x_ref.shape[0]

    def device(chip, which_core):
        return (chip * 2 + which_core, index)

    def in_group(step):
        return group * GROUP + (member + step) % GROUP

    ahead = (rows_at, (index + 1) % n_pairs)
    behind = (rows_at, (index + n_pairs - 1) % n_pairs)
    across = jnp.where(member < 2, z + n_chips // 2 + 2, z + n_chips // 2 - 2) % n_chips
    far = (
        across,
        (z + GROUP) % n_chips,
        (z + n_chips - GROUP) % n_chips,
    )
    near = [device(in_group(step), (core + turn) % 2) for step, turn in HOPS]
    peers = [ahead, behind] + near + [device(chip, core) for chip in far]

    barrier = pltpu.get_barrier_semaphore()
    for peer in peers:
        pl.semaphore_signal(barrier, inc=1, device_id=peer, device_id_type=MESH)
    loads = [
        pltpu.make_async_copy(
            x_ref.at[:, pl.ds(s * BLK, BLK)], first.at[s], in_sem.at[s]
        )
        for s in range(SLOTS)
    ]
    for load in loads:
        load.start()
    for load in loads:
        load.wait()

    def remote(src, dst, send_sem, recv_sem, to):
        return pltpu.make_async_remote_copy(
            src_ref=src, dst_ref=dst, send_sem=send_sem, recv_sem=recv_sem,
            device_id=to, device_id_type=MESH,
        )

    chunk = 8
    steps = local_rows // chunk
    shape = (chunk, LANES)
    reverse = LANES - 1 - lane_of(shape)
    started = []
    pl.semaphore_wait(barrier, len(peers))

    for rnd in range(ROUNDS):
        held = (first, second)[rnd]
        to_ahead = jnp.int32(0)
        to_behind = jnp.int32(0)
        for s in range(SLOTS):
            took = plan_ref[rnd, ahead[1] * SLOTS + s] - index * SLOTS
            to_ahead = jnp.where((took >= 0) & (took < SLOTS), took, to_ahead)
            took = plan_ref[rnd, behind[1] * SLOTS + s] - index * SLOTS
            to_behind = jnp.where((took >= 0) & (took < SLOTS), took, to_behind)
        sent[rnd, 0] = held[to_ahead]
        sent[rnd, 1] = held[to_behind]
        moves = [
            remote(sent.at[rnd, 0], came.at[rnd, 0], block_out.at[rnd, 0], block_in.at[rnd, 0], ahead),
            remote(sent.at[rnd, 1], came.at[rnd, 1], block_out.at[rnd, 1], block_in.at[rnd, 1], behind),
        ]
        for move in moves:
            move.start()
        for move in moves:
            move.wait_recv()
        started += moves

        for pair in range(2):
            at = []
            for side in range(2):
                took = plan_ref[rnd, index * SLOTS + 2 * pair + side] - index * SLOTS
                at.append(took)

            def add_rows(i, acc, pair=pair, at=at, rnd=rnd, held=held):
                rows = pl.ds(pl.multiple_of(i * chunk, chunk), chunk)
                blocks = [
                    jnp.where(
                        took < 0,
                        came[rnd, 0, rows, :],
                        jnp.where(took >= SLOTS, came[rnd, 1, rows, :], held[jnp.clip(took, 0, SLOTS - 1), rows, :]),
                    )
                    for took in at
                ]
                top, bottom, terms = band_terms(*blocks, reverse)
                sides[pair, 0, rows, :] = top
                sides[pair, 1, rows, :] = bottom
                return tuple(a + t for a, t in zip(acc, terms))

            acc = lax.fori_loop(0, steps, add_rows, (jnp.zeros(shape, F32),) * 16)
            for k in range(16):
                bands[rnd, pair, k : k + 1] = jnp.sum(acc[k], axis=0, keepdims=True)

        for k, (step, turn) in enumerate(HOPS):
            there = (core + turn) % 2
            copy = remote(
                bands.at[rnd, there], parts.at[rnd, member * 2 + core],
                part_out.at[rnd, k], part_in.at[rnd, k], device(in_group(step), there),
            )
            copy.start()
            started.append(copy)
        parts[rnd, member * 2 + core] = bands[rnd, core]
        for k, (step, turn) in enumerate(HOPS):
            source = (in_group(GROUP - step) % GROUP) * 2 + (core + turn) % 2
            remote(
                bands.at[rnd, core], parts.at[rnd, source],
                part_out.at[rnd, k], part_in.at[rnd, k], device(in_group(GROUP - step), (core + turn) % 2),
            ).wait_recv()
        total = parts[rnd, 0]
        for k in range(1, 2 * GROUP):
            total = total + parts[rnd, k]
        sums[rnd, group] = total

        for k, chip in enumerate(far):
            copy = remote(
                sums.at[rnd, group], sums.at[rnd, group],
                sum_out.at[rnd, k], sum_in.at[rnd, k], device(chip, core),
            )
            copy.start()
            started.append(copy)
        for k, chip in enumerate((far[0], far[2], far[1])):
            remote(
                sums.at[rnd, group], sums.at[rnd, chip // GROUP],
                sum_out.at[rnd, k], sum_in.at[rnd, k], device(chip, core),
            ).wait_recv()
        total = sums[rnd, 0]
        for k in range(1, n_chips // GROUP):
            total = total + sums[rnd, k]

        entries[...] = jnp.zeros(entries.shape, F32)
        for k in range(4):
            entries[k, 0:4] = total[4 * k : 4 * k + 4]
        entries[2, 0:1] = total[4:5]
        for k in range(4):
            entries[k, 4:5] = roll(jnp.broadcast_to(total[8:9], shape), -8 * k)[0:1]
        cosines, sines = angles(entries[0], entries[1], entries[2], entries[3])
        for k in range(STEPS):
            turns[rnd, core, k : k + 1] = cosines[k]
            turns[rnd, core, STEPS + k : STEPS + k + 1] = sines[k]
        other = device(z, 1 - core)
        copy = remote(turns.at[rnd, core], turns.at[rnd, core], turn_out.at[rnd], turn_in.at[rnd], other)
        copy.start()
        started.append(copy)
        remote(
            turns.at[rnd, core], turns.at[rnd, 1 - core], turn_out.at[rnd], turn_in.at[rnd], other
        ).wait_recv()

        for pair in range(2):
            lines = [jnp.broadcast_to(turns[rnd, pair, k : k + 1], shape) for k in range(2 * STEPS)]

            def turn_rows(i, carry, pair=pair, lines=lines, rnd=rnd):
                rows = pl.ds(pl.multiple_of(i * chunk, chunk), chunk)
                left, right = apply_steps(
                    sides[pair, 0, rows, :], sides[pair, 1, rows, :], lines[:STEPS], lines[STEPS:]
                )
                if rnd < ROUNDS - 1:
                    second[2 * pair, rows, :] = left
                    second[2 * pair + 1, rows, :] = right
                else:
                    result[2 * pair, rows, :] = left
                    result[2 * pair + 1, rows, :] = right
                return carry

            lax.fori_loop(0, steps, turn_rows, 0)

    stores = [
        pltpu.make_async_copy(result.at[s], o_ref.at[:, pl.ds(s * BLK, BLK)], out_sem.at[s])
        for s in range(SLOTS)
    ]
    for store in stores:
        store.start()
    for copy in started:
        copy.wait_send()
    for store in stores:
        store.wait()


def on_device(n_rows, n_pairs, matrix, plan):
    rows, cols = matrix.shape
    dma = pltpu.SemaphoreType.DMA
    near, far = len(HOPS), n_rows // 2 // GROUP - 1
    return pl.pallas_call(
        functools.partial(kernel, n_rows, n_pairs),
        out_shape=jax.ShapeDtypeStruct((rows, cols), F32),
        in_specs=[
            pl.BlockSpec(memory_space=pltpu.SMEM),
            pl.BlockSpec(memory_space=pl.ANY),
        ],
        out_specs=pl.BlockSpec(memory_space=pl.ANY),
        scratch_shapes=[
            pltpu.VMEM((SLOTS, rows, BLK), F32),
            pltpu.VMEM((SLOTS, rows, BLK), F32),
            pltpu.VMEM((ROUNDS, 2, rows, BLK), F32),
            pltpu.VMEM((ROUNDS, 2, rows, BLK), F32),
            pltpu.VMEM((2, 2, rows, BLK), F32),
            pltpu.VMEM((SLOTS, rows, BLK), F32),
            pltpu.VMEM((ROUNDS, 2, 16, BLK), F32),
            pltpu.VMEM((ROUNDS, 2 * GROUP, 16, BLK), F32),
            pltpu.VMEM((ROUNDS, far + 1, 16, BLK), F32),
            pltpu.VMEM((4, 8, BLK), F32),
            pltpu.VMEM((ROUNDS, 2, 2 * STEPS, BLK), F32),
            dma((SLOTS,)),
            dma((SLOTS,)),
            dma((ROUNDS, 2)),
            dma((ROUNDS, 2)),
            dma((ROUNDS, near)),
            dma((ROUNDS, near)),
            dma((ROUNDS, far)),
            dma((ROUNDS, far)),
            dma((ROUNDS,)),
            dma((ROUNDS,)),
        ],
        compiler_params=pltpu.CompilerParams(
            collective_id=0, has_side_effects=True, vmem_limit_bytes=32 * 1024 * 1024
        ),
    )(plan, matrix)


def solution(mesh):
    return jax.shard_map(
        functools.partial(on_device, mesh.shape["rows"], mesh.shape["pairs"]),
        mesh=mesh,
        in_specs=(P("rows", "pairs"), P()),
        out_specs=P("rows", "pairs"),
        check_vma=False,
    )
```

time: 880 us -> 79.4 us (0.09); the launches traced: 864 us -> 79.3 us
  waiting for transfers between devices: 436 us -> 0 us
  local copies, waits for them, and re-layouts: 388 us -> 2.33 us
  Pallas kernels: 0 us -> 76.9 us
  between operations: 15 us -> 0.01 us
  starting transfers between devices: 11.4 us -> 0 us
    psum x2 -> x0, waiting for transfers between devices: 429 us -> none  [on_device(): gram_mat = lax.psum(local_gram, 'rows')]
    slice x142 -> x0, local copies, waits for them, and re-layouts: 239 us -> none  [the longest x109 123 us: take_static(): lax.slice_in_dim(array_in, begin, begin + last - first + 1, axis=axis_no)]
    concatenate x12 -> x0, local copies, waits for them, and re-layouts: 101 us -> none  [take_static(): return jnp.concatenate(pieces, axis=axis_no)]
    pallas_call x0 -> x1, Pallas kernels: none -> 76.9 us  [on_device(): pl.pallas_call(functools.partial(kernel, n_rows, n_pairs), out_shape=jax....]
    gather x48 -> x0, local copies, waits for them, and re-layouts: 44.4 us -> none  [the longest x16 14.8 us: rotate_gram(): jnp.diagonal(current[:, :half_cols, half_cols:], axis1=1, axis2=2)]
    ppermute x4 -> x0, starting transfers between devices: 11.3 us -> none  [from_behind(): return lax.ppermute(block, axis, route)]
  transfers between devices with their start and end apart: 6 -> 0, of which waited for: 6 -> 0; matrix products, arithmetic and copies ran while one was open for 0% -> 0% of each run, Pallas kernels for 0% -> 0%
where the time goes in v1:
time: 79.4 us; the launch traced here: 79.3 us
  Pallas kernels  76.9 us (97%)
  local copies, waits for them, and re-layouts  2.33 us (3%)
    pallas_call x1, Pallas kernels, on_device(): pl.pallas_call(functools.partial(kernel, n_rows, n_pairs), out_shape=jax....  76.9 us
    unnamed x5, local copies, waits for them, and re-layouts  2.33 us

profile of v1, /device:TPU:1, one launch (start us, length us, event | category | flops | bytes accessed | tf_op | source)
XLA Modules:
  0.0 79.3 jit_solution(12422832739296900320)
XLA Ops:
  0.0 0.0 copy-start
  0.0 0.9 %copy-done = f32[128,512]{1,0:T(8,128)S(1)} copy-done((f32[128,512]{1,0:T(8,128)S(1)}, f32[128,512]{1,0:T(8,128)}, u32[]{:S(2)}) %copy-start) | copy-done | bytes 262168
  1.0 0.0 copy-start.1
  1.0 0.7 copy-done.1
  1.6 76.9 %shard_map.28 = f32[128,512]{1,0:T(8,128)S(1)} custom-call(s32[2,64]{1,0:T(2,128)S(1)} %copy-done.1, f32[128,512]{1,0:T(8,128)S(1)} %copy-done), custom_call_target="tpu_custom_call" | custom-call | tf_op jit(solution)/shard_map/pallas_call | solution.py:354
  78.6 0.7 copy.4
Async XLA Ops:
  0.0 0.9 %copy-start = (f32[128,512]{1,0:T(8,128)S(1)}, f32[128,512]{1,0:T(8,128)}, u32[]{:S(2)}) copy-start(f32[128,512]{1,0:T(8,128)} %x_ref.1) | copy-start | bytes 786436
  1.0 0.7 copy-start.1

commit v2 on v1

--- a/solution.py
+++ b/solution.py
@@ -48,6 +48,13 @@
     terms = [top * t for t in tops] + [top * b for b in bottoms]
     terms += [one * two] + [bottom * t for t in tops[1:]] + [bottom * b for b in bottoms]
     return top, bottom, terms
+
+
+def fold(x):
+    total = x[0:8]
+    for first in range(8, x.shape[0], 8):
+        total = total + x[first : first + 8]
+    return total
 
 
 def tangent_of(upper_a, lower_b, coupling):
@@ -162,9 +169,9 @@
 
 
 def kernel(
-    n_rows, n_pairs, plan_ref, x_ref, o_ref,
-    first, second, came, sent, sides, result, bands, parts, sums, entries, turns,
-    in_sem, out_sem, block_out, block_in, part_out, part_in, sum_out, sum_in, turn_out, turn_in,
+    n_rows, n_pairs, plan_in, x_ref, o_ref,
+    first, second, came, sent, sides, result, bands, parts, sums, entries, turns, plan_ref,
+    plan_sem, ready_sem, in_sem, out_sem, block_out, block_in, part_out, part_in, sum_out, sum_in, turn_out, turn_in,
 ):
     rows_at = lax.axis_index("rows")
     index = lax.axis_index("pairs")
@@ -188,12 +195,14 @@
         (z + n_chips - GROUP) % n_chips,
     )
     near = [device(in_group(step), (core + turn) % 2) for step, turn in HOPS]
-    peers = [ahead, behind] + near + [device(chip, core) for chip in far]
+    line = [device((z + step + n_chips) % n_chips, core) for step in (1, -1, 2, -2, 3, -3)]
+    siblings = [device(z, 1 - core)] + [device(in_group(step), 1 - core) for step in (1, 2, 3)]
+    peers = line + siblings + [ahead, behind]
 
     barrier = pltpu.get_barrier_semaphore()
     for peer in peers:
         pl.semaphore_signal(barrier, inc=1, device_id=peer, device_id_type=MESH)
-    loads = [
+    loads = [pltpu.make_async_copy(plan_in, plan_ref, plan_sem)] + [
         pltpu.make_async_copy(
             x_ref.at[:, pl.ds(s * BLK, BLK)], first.at[s], in_sem.at[s]
         )
@@ -210,12 +219,13 @@
             device_id=to, device_id_type=MESH,
         )
 
-    chunk = 8
-    steps = local_rows // chunk
-    shape = (chunk, LANES)
-    reverse = LANES - 1 - lane_of(shape)
+    shape = (8, LANES)
+    gram_rows, turn_chunk = 128, 128
+    reverse = LANES - 1 - lane_of((gram_rows, LANES))
     started = []
     pl.semaphore_wait(barrier, len(peers))
+    for peer in line[2:]:
+        pl.semaphore_signal(ready_sem, inc=1, device_id=peer, device_id_type=MESH)
 
     for rnd in range(ROUNDS):
         held = (first, second)[rnd]
@@ -245,7 +255,7 @@
                 at.append(took)
 
             def add_rows(i, acc, pair=pair, at=at, rnd=rnd, held=held):
-                rows = pl.ds(pl.multiple_of(i * chunk, chunk), chunk)
+                rows = pl.ds(pl.multiple_of(i * gram_rows, gram_rows), gram_rows)
                 blocks = [
                     jnp.where(
                         took < 0,
@@ -257,9 +267,9 @@
                 top, bottom, terms = band_terms(*blocks, reverse)
                 sides[pair, 0, rows, :] = top
                 sides[pair, 1, rows, :] = bottom
-                return tuple(a + t for a, t in zip(acc, terms))
-
-            acc = lax.fori_loop(0, steps, add_rows, (jnp.zeros(shape, F32),) * 16)
+                return tuple(a + fold(t) for a, t in zip(acc, terms))
+
+            acc = lax.fori_loop(0, local_rows // gram_rows, add_rows, (jnp.zeros(shape, F32),) * 16)
             for k in range(16):
                 bands[rnd, pair, k : k + 1] = jnp.sum(acc[k], axis=0, keepdims=True)
 
@@ -283,6 +293,8 @@
             total = total + parts[rnd, k]
         sums[rnd, group] = total
 
+        if rnd == 0:
+            pl.semaphore_wait(ready_sem, len(line[2:]))
         for k, chip in enumerate(far):
             copy = remote(
                 sums.at[rnd, group], sums.at[rnd, group],
@@ -318,10 +330,10 @@
         ).wait_recv()
 
         for pair in range(2):
-            lines = [jnp.broadcast_to(turns[rnd, pair, k : k + 1], shape) for k in range(2 * STEPS)]
+            lines = [jnp.broadcast_to(turns[rnd, pair, k : k + 1], (turn_chunk, LANES)) for k in range(2 * STEPS)]
 
             def turn_rows(i, carry, pair=pair, lines=lines, rnd=rnd):
-                rows = pl.ds(pl.multiple_of(i * chunk, chunk), chunk)
+                rows = pl.ds(pl.multiple_of(i * turn_chunk, turn_chunk), turn_chunk)
                 left, right = apply_steps(
                     sides[pair, 0, rows, :], sides[pair, 1, rows, :], lines[:STEPS], lines[STEPS:]
                 )
@@ -333,7 +345,7 @@
                     result[2 * pair + 1, rows, :] = right
                 return carry
 
-            lax.fori_loop(0, steps, turn_rows, 0)
+            lax.fori_loop(0, local_rows // turn_chunk, turn_rows, 0)
 
     stores = [
         pltpu.make_async_copy(result.at[s], o_ref.at[:, pl.ds(s * BLK, BLK)], out_sem.at[s])
@@ -355,7 +367,7 @@
         functools.partial(kernel, n_rows, n_pairs),
         out_shape=jax.ShapeDtypeStruct((rows, cols), F32),
         in_specs=[
-            pl.BlockSpec(memory_space=pltpu.SMEM),
+            pl.BlockSpec(memory_space=pl.ANY),
             pl.BlockSpec(memory_space=pl.ANY),
         ],
         out_specs=pl.BlockSpec(memory_space=pl.ANY),
@@ -371,6 +383,9 @@
             pltpu.VMEM((ROUNDS, far + 1, 16, BLK), F32),
             pltpu.VMEM((4, 8, BLK), F32),
             pltpu.VMEM((ROUNDS, 2, 2 * STEPS, BLK), F32),
+            pltpu.SMEM((ROUNDS, n_pairs * SLOTS), jnp.int32),
+            dma(()),
+            pltpu.SemaphoreType.REGULAR,
             dma((SLOTS,)),
             dma((SLOTS,)),
             dma((ROUNDS, 2)),
@@ -383,7 +398,7 @@
             dma((ROUNDS,)),
         ],
         compiler_params=pltpu.CompilerParams(
-            collective_id=0, has_side_effects=True, vmem_limit_bytes=32 * 1024 * 1024
+            collective_id=0, has_side_effects=True, vmem_limit_bytes=60 * 1024 * 1024
         ),
     )(plan, matrix)
 

time: 79.4 us -> 51.7 us (0.65)
  Pallas kernels: 76.9 us -> 49.8 us
    pallas_call x1, Pallas kernels: 76.9 us -> 49.8 us  [on_device(): pl.pallas_call(functools.partial(kernel, n_rows, n_pairs), out_shape=jax....]
    unnamed x5 -> x1, local copies, waits for them, and re-layouts: 2.33 us -> 1.67 us
where the time goes in v2:
time: 51.7 us; the launch traced here: 51.5 us
  Pallas kernels  49.8 us (96%)
  local copies, waits for them, and re-layouts  1.67 us (3%)
    pallas_call x1, Pallas kernels, on_device(): pl.pallas_call(functools.partial(kernel, n_rows, n_pairs), out_shape=jax....  49.8 us
    unnamed x1, local copies, waits for them, and re-layouts  1.67 us

profile of v2, /device:TPU:1, one launch (start us, length us, event | category | flops | bytes accessed | tf_op | source)
XLA Modules:
  0.0 51.5 jit_solution(16186988223390667271)
XLA Ops:
  0.0 49.8 %shard_map.28 = f32[128,512]{1,0:T(8,128)} custom-call(s32[2,64]{1,0:T(2,128)} %plan_in.1, f32[128,512]{1,0:T(8,128)} %x_ref.1), custom_call_target="tpu_custom_call" | custom-call | tf_op jit(solution)/shard_map/pallas_call | solution.py:366
  49.8 1.7 %copy.4 = f32[128,512]{1,0:T(8,128)} copy(f32[128,512]{1,0:T(8,128)} %shard_map.28) | data formatting | bytes 524288

commit v3 on v2

--- a/solution.py
+++ b/solution.py
@@ -170,8 +170,9 @@
 
 def kernel(
     n_rows, n_pairs, plan_in, x_ref, o_ref,
-    first, second, came, sent, sides, result, bands, parts, sums, entries, turns, plan_ref,
-    plan_sem, ready_sem, in_sem, out_sem, block_out, block_in, part_out, part_in, sum_out, sum_in, turn_out, turn_in,
+    first, second, third, came, sent, cross, crossed, sides, bands, parts, sums, both, entries, turns, far_turns, last_turns,
+    plan_ref, plan_sem, ready_sem, in_sem, block_out, block_in, cross_out, cross_in, part_out, part_in,
+    sum_out, sum_in, both_out, both_in, turn_out, turn_in,
 ):
     rows_at = lax.axis_index("rows")
     index = lax.axis_index("pairs")
@@ -195,10 +196,9 @@
         (z + n_chips - GROUP) % n_chips,
     )
     near = [device(in_group(step), (core + turn) % 2) for step, turn in HOPS]
-    line = [device((z + step + n_chips) % n_chips, core) for step in (1, -1, 2, -2, 3, -3)]
-    siblings = [device(z, 1 - core)] + [device(in_group(step), 1 - core) for step in (1, 2, 3)]
-    peers = line + siblings + [ahead, behind]
-
+    line = [device((z + step + n_chips) % n_chips, core) for step in (1, -1, 2, -2)]
+    other = device(z, 1 - core)
+    peers = line[:2] + [ahead, behind, other]
     barrier = pltpu.get_barrier_semaphore()
     for peer in peers:
         pl.semaphore_signal(barrier, inc=1, device_id=peer, device_id_type=MESH)
@@ -220,59 +220,40 @@
         )
 
     shape = (8, LANES)
-    gram_rows, turn_chunk = 128, 128
-    reverse = LANES - 1 - lane_of((gram_rows, LANES))
+    reverse = LANES - 1 - lane_of((local_rows, LANES))
     started = []
     pl.semaphore_wait(barrier, len(peers))
-    for peer in line[2:]:
-        pl.semaphore_signal(ready_sem, inc=1, device_id=peer, device_id_type=MESH)
-
-    for rnd in range(ROUNDS):
-        held = (first, second)[rnd]
-        to_ahead = jnp.int32(0)
-        to_behind = jnp.int32(0)
+
+    def here(level, to):
+        for peer in to:
+            pl.semaphore_signal(ready_sem.at[level], inc=1, device_id=peer, device_id_type=MESH)
+
+    def known(level):
+        pl.semaphore_wait(ready_sem.at[level], 2)
+
+    here(0, line[:2])
+
+    def slots_taken(rnd, at):
+        taken = jnp.int32(0)
         for s in range(SLOTS):
-            took = plan_ref[rnd, ahead[1] * SLOTS + s] - index * SLOTS
-            to_ahead = jnp.where((took >= 0) & (took < SLOTS), took, to_ahead)
-            took = plan_ref[rnd, behind[1] * SLOTS + s] - index * SLOTS
-            to_behind = jnp.where((took >= 0) & (took < SLOTS), took, to_behind)
-        sent[rnd, 0] = held[to_ahead]
-        sent[rnd, 1] = held[to_behind]
-        moves = [
-            remote(sent.at[rnd, 0], came.at[rnd, 0], block_out.at[rnd, 0], block_in.at[rnd, 0], ahead),
-            remote(sent.at[rnd, 1], came.at[rnd, 1], block_out.at[rnd, 1], block_in.at[rnd, 1], behind),
-        ]
-        for move in moves:
-            move.start()
-        for move in moves:
-            move.wait_recv()
-        started += moves
-
+            took = plan_ref[rnd, at * SLOTS + s] - index * SLOTS
+            taken = jnp.where((took >= 0) & (took < SLOTS), took, taken)
+        return taken
+
+    def band_sums(rnd, held, came):
         for pair in range(2):
-            at = []
+            blocks = []
             for side in range(2):
                 took = plan_ref[rnd, index * SLOTS + 2 * pair + side] - index * SLOTS
-                at.append(took)
-
-            def add_rows(i, acc, pair=pair, at=at, rnd=rnd, held=held):
-                rows = pl.ds(pl.multiple_of(i * gram_rows, gram_rows), gram_rows)
-                blocks = [
-                    jnp.where(
-                        took < 0,
-                        came[rnd, 0, rows, :],
-                        jnp.where(took >= SLOTS, came[rnd, 1, rows, :], held[jnp.clip(took, 0, SLOTS - 1), rows, :]),
-                    )
-                    for took in at
-                ]
-                top, bottom, terms = band_terms(*blocks, reverse)
-                sides[pair, 0, rows, :] = top
-                sides[pair, 1, rows, :] = bottom
-                return tuple(a + fold(t) for a, t in zip(acc, terms))
-
-            acc = lax.fori_loop(0, local_rows // gram_rows, add_rows, (jnp.zeros(shape, F32),) * 16)
+                own = held[jnp.clip(took, 0, SLOTS - 1)]
+                blocks.append(jnp.where(took < 0, came[0], jnp.where(took >= SLOTS, came[1], own)))
+            top, bottom, terms = band_terms(*blocks, reverse)
+            sides[pair, 0] = top
+            sides[pair, 1] = bottom
             for k in range(16):
-                bands[rnd, pair, k : k + 1] = jnp.sum(acc[k], axis=0, keepdims=True)
-
+                bands[rnd, pair, k : k + 1] = jnp.sum(fold(terms[k]), axis=0, keepdims=True)
+
+    def group_sums(rnd):
         for k, (step, turn) in enumerate(HOPS):
             there = (core + turn) % 2
             copy = remote(
@@ -282,6 +263,8 @@
             copy.start()
             started.append(copy)
         parts[rnd, member * 2 + core] = bands[rnd, core]
+
+    def group_total(rnd):
         for k, (step, turn) in enumerate(HOPS):
             source = (in_group(GROUP - step) % GROUP) * 2 + (core + turn) % 2
             remote(
@@ -291,72 +274,133 @@
         total = parts[rnd, 0]
         for k in range(1, 2 * GROUP):
             total = total + parts[rnd, k]
-        sums[rnd, group] = total
-
-        if rnd == 0:
-            pl.semaphore_wait(ready_sem, len(line[2:]))
-        for k, chip in enumerate(far):
-            copy = remote(
-                sums.at[rnd, group], sums.at[rnd, group],
-                sum_out.at[rnd, k], sum_in.at[rnd, k], device(chip, core),
-            )
-            copy.start()
-            started.append(copy)
-        for k, chip in enumerate((far[0], far[2], far[1])):
-            remote(
-                sums.at[rnd, group], sums.at[rnd, chip // GROUP],
-                sum_out.at[rnd, k], sum_in.at[rnd, k], device(chip, core),
-            ).wait_recv()
-        total = sums[rnd, 0]
+        return total
+
+    def full_total(ref):
+        total = ref[0]
         for k in range(1, n_chips // GROUP):
-            total = total + sums[rnd, k]
-
-        entries[...] = jnp.zeros(entries.shape, F32)
+            total = total + ref[k]
+        return total
+
+    def angles_of(total, work):
+        work[...] = jnp.zeros(work.shape, F32)
         for k in range(4):
-            entries[k, 0:4] = total[4 * k : 4 * k + 4]
-        entries[2, 0:1] = total[4:5]
+            work[k, 0:4] = total[4 * k : 4 * k + 4]
+        work[2, 0:1] = total[4:5]
         for k in range(4):
-            entries[k, 4:5] = roll(jnp.broadcast_to(total[8:9], shape), -8 * k)[0:1]
-        cosines, sines = angles(entries[0], entries[1], entries[2], entries[3])
-        for k in range(STEPS):
-            turns[rnd, core, k : k + 1] = cosines[k]
-            turns[rnd, core, STEPS + k : STEPS + k + 1] = sines[k]
-        other = device(z, 1 - core)
-        copy = remote(turns.at[rnd, core], turns.at[rnd, core], turn_out.at[rnd], turn_in.at[rnd], other)
+            work[k, 4:5] = roll(jnp.broadcast_to(total[8:9], shape), -8 * k)[0:1]
+        return angles(work[0], work[1], work[2], work[3])
+
+    def spread(x):
+        return jnp.broadcast_to(x, (local_rows, LANES))
+
+    def turned(top, bottom, lines):
+        wide = [spread(line) for line in lines]
+        return apply_steps(top, bottom, wide[:STEPS], wide[STEPS:])
+
+    sent[0] = first[slots_taken(0, ahead[1])]
+    sent[1] = first[slots_taken(0, behind[1])]
+    moves = [
+        remote(sent.at[0], came.at[0], block_out.at[0], block_in.at[0], ahead),
+        remote(sent.at[1], came.at[1], block_out.at[1], block_in.at[1], behind),
+    ]
+    for move in moves:
+        move.start()
+    known(0)
+    here(1, line[2:])
+    known(1)
+    here(2, line[2:])
+    for move in moves:
+        move.wait_recv()
+    started += moves
+    band_sums(0, first, came)
+    group_sums(0)
+
+    for way, to in enumerate((ahead, behind)):
+        from_second = slots_taken(1, to[1]) >= 2
+        for side in range(2):
+            cross[way, side] = jnp.where(from_second, sides[1, side], sides[0, side])
+        move = remote(cross.at[way], crossed.at[way], cross_out.at[way], cross_in.at[way], to)
+        move.start()
+        moves.append(move)
+    started += moves[2:]
+
+    sums[group] = group_total(0)
+    known(2)
+    for k, chip in enumerate(far):
+        copy = remote(sums.at[group], sums.at[group], sum_out.at[k], sum_in.at[k], device(chip, core))
         copy.start()
         started.append(copy)
+    for k, chip in enumerate((far[0], far[2], far[1])):
         remote(
-            turns.at[rnd, core], turns.at[rnd, 1 - core], turn_out.at[rnd], turn_in.at[rnd], other
+            sums.at[group], sums.at[chip // GROUP], sum_out.at[k], sum_in.at[k], device(chip, core)
         ).wait_recv()
-
-        for pair in range(2):
-            lines = [jnp.broadcast_to(turns[rnd, pair, k : k + 1], (turn_chunk, LANES)) for k in range(2 * STEPS)]
-
-            def turn_rows(i, carry, pair=pair, lines=lines, rnd=rnd):
-                rows = pl.ds(pl.multiple_of(i * turn_chunk, turn_chunk), turn_chunk)
-                left, right = apply_steps(
-                    sides[pair, 0, rows, :], sides[pair, 1, rows, :], lines[:STEPS], lines[STEPS:]
-                )
-                if rnd < ROUNDS - 1:
-                    second[2 * pair, rows, :] = left
-                    second[2 * pair + 1, rows, :] = right
-                else:
-                    result[2 * pair, rows, :] = left
-                    result[2 * pair + 1, rows, :] = right
-                return carry
-
-            lax.fori_loop(0, local_rows // turn_chunk, turn_rows, 0)
-
-    stores = [
-        pltpu.make_async_copy(result.at[s], o_ref.at[:, pl.ds(s * BLK, BLK)], out_sem.at[s])
-        for s in range(SLOTS)
-    ]
-    for store in stores:
-        store.start()
+    cosines, sines = angles_of(full_total(sums), entries.at[0])
+    for k in range(STEPS):
+        turns[core, k : k + 1] = cosines[k]
+        turns[core, STEPS + k : STEPS + k + 1] = sines[k]
+    for k, (way, there) in enumerate(((0, 0), (0, 1), (1, 0), (1, 1))):
+        to = (z * 2 + (core + there) % 2, (ahead, behind)[way][1])
+        copy = remote(turns.at[core], far_turns.at[way, core], turn_out.at[k], turn_in.at[k], to)
+        copy.start()
+        started.append(copy)
+    copy = remote(turns.at[core], turns.at[core], turn_out.at[4], turn_in.at[4], other)
+    copy.start()
+    started.append(copy)
+    remote(turns.at[core], turns.at[1 - core], turn_out.at[4], turn_in.at[4], other).wait_recv()
+    for pair in range(2):
+        lines = [turns[pair, k : k + 1] for k in range(2 * STEPS)]
+        left, right = turned(sides[pair, 0], sides[pair, 1], lines)
+        second[2 * pair] = left
+        second[2 * pair + 1] = right
+    for k, (way, there) in enumerate(((0, 0), (0, 1), (1, 0), (1, 1))):
+        source = (z * 2 + (core + there) % 2, (behind, ahead)[way][1])
+        remote(
+            turns.at[core], far_turns.at[way, (core + there) % 2], turn_out.at[k], turn_in.at[k], source
+        ).wait_recv()
+    for move in moves[2:]:
+        move.wait_recv()
+    for way in range(2):
+        took = jnp.int32(0)
+        for s in range(SLOTS):
+            at = plan_ref[1, index * SLOTS + s] - index * SLOTS + (SLOTS, -SLOTS)[way]
+            took = jnp.where((at >= 0) & (at < SLOTS), at, took)
+        lines = [
+            jnp.where(took >= 2, far_turns[way, 1, k : k + 1], far_turns[way, 0, k : k + 1])
+            for k in range(2 * STEPS)
+        ]
+        left, right = turned(crossed[way, 0], crossed[way, 1], lines)
+        third[way] = jnp.where((took == 1) | (took == 3), right, left)
+
+    band_sums(1, second, third)
+    group_sums(1)
+    both[group] = group_total(1)
+    for k, chip in enumerate(far):
+        copy = remote(
+            both.at[group], both.at[group], both_out.at[k], both_in.at[k], device(chip, core)
+        )
+        copy.start()
+        started.append(copy)
+    for k, chip in enumerate((far[0], far[2], far[1])):
+        remote(
+            both.at[group], both.at[chip // GROUP], both_out.at[k], both_in.at[k], device(chip, core)
+        ).wait_recv()
+    cosines, sines = angles_of(full_total(both), entries.at[1])
+    for k in range(STEPS):
+        last_turns[core, k : k + 1] = cosines[k]
+        last_turns[core, STEPS + k : STEPS + k + 1] = sines[k]
+    copy = remote(last_turns.at[core], last_turns.at[core], turn_out.at[5], turn_in.at[5], other)
+    copy.start()
+    started.append(copy)
+    remote(last_turns.at[core], last_turns.at[1 - core], turn_out.at[5], turn_in.at[5], other).wait_recv()
+    for pair in range(2):
+        lines = [last_turns[pair, k : k + 1] for k in range(2 * STEPS)]
+        left, right = turned(sides[pair, 0], sides[pair, 1], lines)
+        o_ref[:, 2 * pair * BLK : (2 * pair + 1) * BLK] = left
+        o_ref[:, (2 * pair + 1) * BLK : (2 * pair + 2) * BLK] = right
+
     for copy in started:
         copy.wait_send()
-    for store in stores:
-        store.wait()
 
 
 def on_device(n_rows, n_pairs, matrix, plan):
@@ -365,37 +409,45 @@
     near, far = len(HOPS), n_rows // 2 // GROUP - 1
     return pl.pallas_call(
         functools.partial(kernel, n_rows, n_pairs),
-        out_shape=jax.ShapeDtypeStruct((rows, cols), F32),
+        out_shape=pltpu.VMEM((rows, cols), F32),
         in_specs=[
             pl.BlockSpec(memory_space=pl.ANY),
             pl.BlockSpec(memory_space=pl.ANY),
         ],
-        out_specs=pl.BlockSpec(memory_space=pl.ANY),
+        out_specs=pl.BlockSpec(memory_space=pltpu.VMEM),
         scratch_shapes=[
             pltpu.VMEM((SLOTS, rows, BLK), F32),
             pltpu.VMEM((SLOTS, rows, BLK), F32),
-            pltpu.VMEM((ROUNDS, 2, rows, BLK), F32),
-            pltpu.VMEM((ROUNDS, 2, rows, BLK), F32),
+            pltpu.VMEM((2, rows, BLK), F32),
+            pltpu.VMEM((2, rows, BLK), F32),
+            pltpu.VMEM((2, rows, BLK), F32),
             pltpu.VMEM((2, 2, rows, BLK), F32),
-            pltpu.VMEM((SLOTS, rows, BLK), F32),
+            pltpu.VMEM((2, 2, rows, BLK), F32),
+            pltpu.VMEM((2, 2, rows, BLK), F32),
             pltpu.VMEM((ROUNDS, 2, 16, BLK), F32),
             pltpu.VMEM((ROUNDS, 2 * GROUP, 16, BLK), F32),
-            pltpu.VMEM((ROUNDS, far + 1, 16, BLK), F32),
-            pltpu.VMEM((4, 8, BLK), F32),
-            pltpu.VMEM((ROUNDS, 2, 2 * STEPS, BLK), F32),
+            pltpu.VMEM((far + 1, 16, BLK), F32),
+            pltpu.VMEM((far + 1, 16, BLK), F32),
+            pltpu.VMEM((2, 4, 8, BLK), F32),
+            pltpu.VMEM((2, 2 * STEPS, BLK), F32),
+            pltpu.VMEM((2, 2, 2 * STEPS, BLK), F32),
+            pltpu.VMEM((2, 2 * STEPS, BLK), F32),
             pltpu.SMEM((ROUNDS, n_pairs * SLOTS), jnp.int32),
             dma(()),
-            pltpu.SemaphoreType.REGULAR,
+            pltpu.SemaphoreType.REGULAR((3,)),
             dma((SLOTS,)),
-            dma((SLOTS,)),
-            dma((ROUNDS, 2)),
-            dma((ROUNDS, 2)),
+            dma((2,)),
+            dma((2,)),
+            dma((2,)),
+            dma((2,)),
             dma((ROUNDS, near)),
             dma((ROUNDS, near)),
-            dma((ROUNDS, far)),
-            dma((ROUNDS, far)),
-            dma((ROUNDS,)),
-            dma((ROUNDS,)),
+            dma((far,)),
+            dma((far,)),
+            dma((far,)),
+            dma((far,)),
+            dma((6,)),
+            dma((6,)),
         ],
         compiler_params=pltpu.CompilerParams(
             collective_id=0, has_side_effects=True, vmem_limit_bytes=60 * 1024 * 1024

time: 51.7 us -> 48.9 us (0.946)
  Pallas kernels: 49.8 us -> 48 us
  local copies, waits for them, and re-layouts: 1.67 us -> 0.71 us
    pallas_call x1, Pallas kernels: 49.8 us -> 48 us  [on_device(): pl.pallas_call(functools.partial(kernel, n_rows, n_pairs), out_shape=pltp...]
    unnamed x1, local copies, waits for them, and re-layouts: 1.67 us -> 0.71 us
where the time goes in v3:
time: 48.9 us; the launch traced here: 48.8 us
  Pallas kernels  48 us (98%)
  local copies, waits for them, and re-layouts  0.71 us (1%)
    pallas_call x1, Pallas kernels, on_device(): pl.pallas_call(functools.partial(kernel, n_rows, n_pairs), out_shape=pltp...  48 us

profile of v3, /device:TPU:1, one launch (start us, length us, event | category | flops | bytes accessed | tf_op | source)
XLA Modules:
  0.0 48.8 jit_solution(1585870394807552050)
XLA Ops:
  0.0 48.0 %shard_map.28 = f32[128,512]{1,0:T(8,128)S(1)} custom-call(s32[2,64]{1,0:T(2,128)} %plan_in.1, f32[128,512]{1,0:T(8,128)} %x_ref.1), custom_call_target="tpu_custom_call" | custom-call | tf_op jit(solution)/shard_map/pallas_call | solution.py:410
  48.1 0.7 %copy.4 = f32[128,512]{1,0:T(8,128)} copy(f32[128,512]{1,0:T(8,128)S(1)} %shard_map.28) | data formatting | bytes 524288

commit v4 on v3

--- a/solution.py
+++ b/solution.py
@@ -14,8 +14,9 @@
 SLOTS = 4
 GROUP = 4
 LANES = 128
+ENTRIES = 16
 F32 = jnp.float32
-HOPS = ((2, 0), (2, 1), (3, 0), (3, 1), (1, 0), (1, 1), (0, 1))
+HOPS = ((3, 0), (3, 1), (2, 0), (2, 1), (1, 0), (1, 1), (0, 1))
 
 
 def roll(x, by):
@@ -170,9 +171,9 @@
 
 def kernel(
     n_rows, n_pairs, plan_in, x_ref, o_ref,
-    first, second, third, came, sent, cross, crossed, sides, bands, parts, sums, both, entries, turns, far_turns, last_turns,
+    first, second, third, came, sent, cross, crossed, sides, bands, parts, sums, entries, turns, far_turns, last_turns,
     plan_ref, plan_sem, ready_sem, in_sem, block_out, block_in, cross_out, cross_in, part_out, part_in,
-    sum_out, sum_in, both_out, both_in, turn_out, turn_in,
+    sum_out, sum_in, turn_out, turn_in,
 ):
     rows_at = lax.axis_index("rows")
     index = lax.axis_index("pairs")
@@ -184,18 +185,27 @@
     def device(chip, which_core):
         return (chip * 2 + which_core, index)
 
-    def in_group(step):
-        return group * GROUP + (member + step) % GROUP
-
+    partner = [
+        group * GROUP + at
+        for at in (member, member + 1 - 2 * (member % 2), (member + 2) % GROUP, GROUP - 1 - member)
+    ]
+    near = [(which * 2 + turn, (core + turn) % 2, device(partner[which], (core + turn) % 2)) for which, turn in HOPS]
+    near_slot = [
+        ((member // 2 + at // 2) % 2 * 2 + (member + at) % 2) * 2 + (core + which_core) % 2
+        for at in range(GROUP)
+        for which_core in range(2)
+    ]
     ahead = (rows_at, (index + 1) % n_pairs)
     behind = (rows_at, (index + n_pairs - 1) % n_pairs)
     across = jnp.where(member < 2, z + n_chips // 2 + 2, z + n_chips // 2 - 2) % n_chips
-    far = (
-        across,
-        (z + GROUP) % n_chips,
-        (z + n_chips - GROUP) % n_chips,
-    )
-    near = [device(in_group(step), (core + turn) % 2) for step, turn in HOPS]
+    n_groups = n_chips // GROUP
+    far = [(2, device(across, core)), (3, device((z + GROUP) % n_chips, core)), (1, device((z + n_chips - GROUP) % n_chips, core))]
+    far_slot = [(at + n_groups - group) % n_groups for at in range(n_groups)]
+    both_cores = [
+        (way, (rows_at if turn == 0 else z * 2 + 1 - core, to[1]))
+        for way, to in enumerate((ahead, behind))
+        for turn in (0, 1)
+    ]
     line = [device((z + step + n_chips) % n_chips, core) for step in (1, -1, 2, -2)]
     other = device(z, 1 - core)
     peers = line[:2] + [ahead, behind, other]
@@ -221,7 +231,6 @@
 
     shape = (8, LANES)
     reverse = LANES - 1 - lane_of((local_rows, LANES))
-    started = []
     pl.semaphore_wait(barrier, len(peers))
 
     def here(level, to):
@@ -253,33 +262,34 @@
             for k in range(16):
                 bands[rnd, pair, k : k + 1] = jnp.sum(fold(terms[k]), axis=0, keepdims=True)
 
-    def group_sums(rnd):
-        for k, (step, turn) in enumerate(HOPS):
-            there = (core + turn) % 2
-            copy = remote(
-                bands.at[rnd, there], parts.at[rnd, member * 2 + core],
-                part_out.at[rnd, k], part_in.at[rnd, k], device(in_group(step), there),
-            )
-            copy.start()
-            started.append(copy)
-        parts[rnd, member * 2 + core] = bands[rnd, core]
-
-    def group_total(rnd):
-        for k, (step, turn) in enumerate(HOPS):
-            source = (in_group(GROUP - step) % GROUP) * 2 + (core + turn) % 2
+    def wait_all(refs, send_sem, recv_sem):
+        return remote(refs, refs, send_sem, recv_sem, other)
+
+    def send_near(rnd):
+        for slot, there, to in near:
             remote(
-                bands.at[rnd, core], parts.at[rnd, source],
-                part_out.at[rnd, k], part_in.at[rnd, k], device(in_group(GROUP - step), (core + turn) % 2),
-            ).wait_recv()
-        total = parts[rnd, 0]
-        for k in range(1, 2 * GROUP):
-            total = total + parts[rnd, k]
-        return total
-
-    def full_total(ref):
-        total = ref[0]
-        for k in range(1, n_chips // GROUP):
-            total = total + ref[k]
+                bands.at[rnd, there], parts.at[rnd, slot], part_out.at[rnd], part_in.at[rnd], to
+            ).start()
+        parts[rnd, 0] = bands[rnd, core]
+        return wait_all(parts.at[rnd, pl.ds(1, len(near))], part_out.at[rnd], part_in.at[rnd])
+
+    def sum_rows(rnd, near_copies):
+        near_copies.wait_recv()
+        sums[rnd, 0] = in_order(parts.at[rnd], near_slot)
+        if rnd == 0:
+            known(2)
+        for slot, to in far:
+            remote(sums.at[rnd, 0], sums.at[rnd, slot], sum_out.at[rnd], sum_in.at[rnd], to).start()
+        copies = wait_all(sums.at[rnd, pl.ds(1, len(far))], sum_out.at[rnd], sum_in.at[rnd])
+        near_copies.wait_send()
+        copies.wait_recv()
+        total = in_order(sums.at[rnd], far_slot)
+        return total, copies
+
+    def in_order(ref, slots):
+        total = ref[slots[0]]
+        for slot in slots[1:]:
+            total = total + ref[slot]
         return total
 
     def angles_of(total, work):
@@ -298,68 +308,46 @@
         wide = [spread(line) for line in lines]
         return apply_steps(top, bottom, wide[:STEPS], wide[STEPS:])
 
-    sent[0] = first[slots_taken(0, ahead[1])]
-    sent[1] = first[slots_taken(0, behind[1])]
-    moves = [
-        remote(sent.at[0], came.at[0], block_out.at[0], block_in.at[0], ahead),
-        remote(sent.at[1], came.at[1], block_out.at[1], block_in.at[1], behind),
-    ]
-    for move in moves:
-        move.start()
+    for way, to in enumerate((ahead, behind)):
+        sent[way] = first[slots_taken(0, to[1])]
+        remote(sent.at[way], came.at[way], block_out, block_in, to).start()
+    blocks = wait_all(came, block_out, block_in)
     known(0)
     here(1, line[2:])
     known(1)
     here(2, line[2:])
-    for move in moves:
-        move.wait_recv()
-    started += moves
+    blocks.wait_recv()
     band_sums(0, first, came)
-    group_sums(0)
+    near_copies = send_near(0)
 
     for way, to in enumerate((ahead, behind)):
         from_second = slots_taken(1, to[1]) >= 2
         for side in range(2):
             cross[way, side] = jnp.where(from_second, sides[1, side], sides[0, side])
-        move = remote(cross.at[way], crossed.at[way], cross_out.at[way], cross_in.at[way], to)
-        move.start()
-        moves.append(move)
-    started += moves[2:]
-
-    sums[group] = group_total(0)
-    known(2)
-    for k, chip in enumerate(far):
-        copy = remote(sums.at[group], sums.at[group], sum_out.at[k], sum_in.at[k], device(chip, core))
-        copy.start()
-        started.append(copy)
-    for k, chip in enumerate((far[0], far[2], far[1])):
-        remote(
-            sums.at[group], sums.at[chip // GROUP], sum_out.at[k], sum_in.at[k], device(chip, core)
-        ).wait_recv()
-    cosines, sines = angles_of(full_total(sums), entries.at[0])
+        remote(cross.at[way], crossed.at[way], cross_out, cross_in, to).start()
+    columns = wait_all(crossed, cross_out, cross_in)
+    blocks.wait_send()
+
+    total, far_copies = sum_rows(0, near_copies)
+    cosines, sines = angles_of(total, entries.at[0])
     for k in range(STEPS):
         turns[core, k : k + 1] = cosines[k]
         turns[core, STEPS + k : STEPS + k + 1] = sines[k]
-    for k, (way, there) in enumerate(((0, 0), (0, 1), (1, 0), (1, 1))):
-        to = (z * 2 + (core + there) % 2, (ahead, behind)[way][1])
-        copy = remote(turns.at[core], far_turns.at[way, core], turn_out.at[k], turn_in.at[k], to)
-        copy.start()
-        started.append(copy)
-    copy = remote(turns.at[core], turns.at[core], turn_out.at[4], turn_in.at[4], other)
-    copy.start()
-    started.append(copy)
-    remote(turns.at[core], turns.at[1 - core], turn_out.at[4], turn_in.at[4], other).wait_recv()
+    for way, to in both_cores:
+        remote(turns.at[core], far_turns.at[way, core], turn_out.at[0], turn_in.at[0], to).start()
+    far_angles = wait_all(far_turns, turn_out.at[0], turn_in.at[0])
+    remote(turns.at[core], turns.at[core], turn_out.at[1], turn_in.at[1], other).start()
+    angles_here = wait_all(turns.at[1 - core], turn_out.at[1], turn_in.at[1])
+    far_copies.wait_send()
+    columns.wait_send()
+    angles_here.wait_recv()
     for pair in range(2):
         lines = [turns[pair, k : k + 1] for k in range(2 * STEPS)]
         left, right = turned(sides[pair, 0], sides[pair, 1], lines)
         second[2 * pair] = left
         second[2 * pair + 1] = right
-    for k, (way, there) in enumerate(((0, 0), (0, 1), (1, 0), (1, 1))):
-        source = (z * 2 + (core + there) % 2, (behind, ahead)[way][1])
-        remote(
-            turns.at[core], far_turns.at[way, (core + there) % 2], turn_out.at[k], turn_in.at[k], source
-        ).wait_recv()
-    for move in moves[2:]:
-        move.wait_recv()
+    columns.wait_recv()
+    far_angles.wait_recv()
     for way in range(2):
         took = jnp.int32(0)
         for s in range(SLOTS):
@@ -373,40 +361,30 @@
         third[way] = jnp.where((took == 1) | (took == 3), right, left)
 
     band_sums(1, second, third)
-    group_sums(1)
-    both[group] = group_total(1)
-    for k, chip in enumerate(far):
-        copy = remote(
-            both.at[group], both.at[group], both_out.at[k], both_in.at[k], device(chip, core)
-        )
-        copy.start()
-        started.append(copy)
-    for k, chip in enumerate((far[0], far[2], far[1])):
-        remote(
-            both.at[group], both.at[chip // GROUP], both_out.at[k], both_in.at[k], device(chip, core)
-        ).wait_recv()
-    cosines, sines = angles_of(full_total(both), entries.at[1])
+    near_copies = send_near(1)
+    far_angles.wait_send()
+    angles_here.wait_send()
+    total, far_copies = sum_rows(1, near_copies)
+    cosines, sines = angles_of(total, entries.at[1])
     for k in range(STEPS):
         last_turns[core, k : k + 1] = cosines[k]
         last_turns[core, STEPS + k : STEPS + k + 1] = sines[k]
-    copy = remote(last_turns.at[core], last_turns.at[core], turn_out.at[5], turn_in.at[5], other)
-    copy.start()
-    started.append(copy)
-    remote(last_turns.at[core], last_turns.at[1 - core], turn_out.at[5], turn_in.at[5], other).wait_recv()
+    remote(last_turns.at[core], last_turns.at[core], turn_out.at[2], turn_in.at[2], other).start()
+    angles_here = wait_all(last_turns.at[1 - core], turn_out.at[2], turn_in.at[2])
+    far_copies.wait_send()
+    angles_here.wait_recv()
     for pair in range(2):
         lines = [last_turns[pair, k : k + 1] for k in range(2 * STEPS)]
         left, right = turned(sides[pair, 0], sides[pair, 1], lines)
         o_ref[:, 2 * pair * BLK : (2 * pair + 1) * BLK] = left
         o_ref[:, (2 * pair + 1) * BLK : (2 * pair + 2) * BLK] = right
 
-    for copy in started:
-        copy.wait_send()
+    angles_here.wait_send()
 
 
 def on_device(n_rows, n_pairs, matrix, plan):
     rows, cols = matrix.shape
     dma = pltpu.SemaphoreType.DMA
-    near, far = len(HOPS), n_rows // 2 // GROUP - 1
     return pl.pallas_call(
         functools.partial(kernel, n_rows, n_pairs),
         out_shape=pltpu.VMEM((rows, cols), F32),
@@ -424,10 +402,9 @@
             pltpu.VMEM((2, 2, rows, BLK), F32),
             pltpu.VMEM((2, 2, rows, BLK), F32),
             pltpu.VMEM((2, 2, rows, BLK), F32),
-            pltpu.VMEM((ROUNDS, 2, 16, BLK), F32),
-            pltpu.VMEM((ROUNDS, 2 * GROUP, 16, BLK), F32),
-            pltpu.VMEM((far + 1, 16, BLK), F32),
-            pltpu.VMEM((far + 1, 16, BLK), F32),
+            pltpu.VMEM((ROUNDS, 2, ENTRIES, BLK), F32),
+            pltpu.VMEM((ROUNDS, 2 * GROUP, ENTRIES, BLK), F32),
+            pltpu.VMEM((ROUNDS, n_rows // 2 // GROUP, ENTRIES, BLK), F32),
             pltpu.VMEM((2, 4, 8, BLK), F32),
             pltpu.VMEM((2, 2 * STEPS, BLK), F32),
             pltpu.VMEM((2, 2, 2 * STEPS, BLK), F32),
@@ -436,18 +413,16 @@
             dma(()),
             pltpu.SemaphoreType.REGULAR((3,)),
             dma((SLOTS,)),
-            dma((2,)),
-            dma((2,)),
-            dma((2,)),
-            dma((2,)),
-            dma((ROUNDS, near)),
-            dma((ROUNDS, near)),
-            dma((far,)),
-            dma((far,)),
-            dma((far,)),
-            dma((far,)),
-            dma((6,)),
-            dma((6,)),
+            dma(()),
+            dma(()),
+            dma(()),
+            dma(()),
+            dma((ROUNDS,)),
+            dma((ROUNDS,)),
+            dma((ROUNDS,)),
+            dma((ROUNDS,)),
+            dma((3,)),
+            dma((3,)),
         ],
         compiler_params=pltpu.CompilerParams(
             collective_id=0, has_side_effects=True, vmem_limit_bytes=60 * 1024 * 1024

time: 48.9 us -> 48.4 us (0.990)
  Pallas kernels: 48 us -> 47.5 us
    pallas_call x1, Pallas kernels: 48 us -> 47.5 us  [on_device(): pl.pallas_call(functools.partial(kernel, n_rows, n_pairs), out_shape=pltp...]
where the time goes in v4:
time: 48.4 us; the launch traced here: 48.2 us
  Pallas kernels  47.5 us (98%)
  local copies, waits for them, and re-layouts  0.71 us (1%)
    pallas_call x1, Pallas kernels, on_device(): pl.pallas_call(functools.partial(kernel, n_rows, n_pairs), out_shape=pltp...  47.5 us

profile of v4, /device:TPU:1, one launch (start us, length us, event | category | flops | bytes accessed | tf_op | source)
XLA Modules:
  0.0 48.2 jit_solution(16065307720175016830)
XLA Ops:
  0.0 47.5 %shard_map.28 = f32[128,512]{1,0:T(8,128)S(1)} custom-call(s32[2,64]{1,0:T(2,128)} %plan_in.1, f32[128,512]{1,0:T(8,128)} %x_ref.1), custom_call_target="tpu_custom_call" | custom-call | tf_op jit(solution)/shard_map/pallas_call | solution.py:388
  47.5 0.7 %copy.4 = f32[128,512]{1,0:T(8,128)} copy(f32[128,512]{1,0:T(8,128)S(1)} %shard_map.28) | data formatting | bytes 524288

commit v5 on v4

--- a/solution.py
+++ b/solution.py
@@ -173,7 +173,7 @@
     n_rows, n_pairs, plan_in, x_ref, o_ref,
     first, second, third, came, sent, cross, crossed, sides, bands, parts, sums, entries, turns, far_turns, last_turns,
     plan_ref, plan_sem, ready_sem, in_sem, block_out, block_in, cross_out, cross_in, part_out, part_in,
-    sum_out, sum_in, turn_out, turn_in,
+    sum_out, sum_in, far_turn_out, far_turn_in, turn_out, turn_in,
 ):
     rows_at = lax.axis_index("rows")
     index = lax.axis_index("pairs")
@@ -201,17 +201,20 @@
     n_groups = n_chips // GROUP
     far = [(2, device(across, core)), (3, device((z + GROUP) % n_chips, core)), (1, device((z + n_chips - GROUP) % n_chips, core))]
     far_slot = [(at + n_groups - group) % n_groups for at in range(n_groups)]
-    both_cores = [
-        (way, (rows_at if turn == 0 else z * 2 + 1 - core, to[1]))
-        for way, to in enumerate((ahead, behind))
-        for turn in (0, 1)
-    ]
+    has = (index < n_pairs - 1, index > 0)
+    sides_here = has[::-1]
     line = [device((z + step + n_chips) % n_chips, core) for step in (1, -1, 2, -2)]
     other = device(z, 1 - core)
-    peers = line[:2] + [ahead, behind, other]
+    peers = line[:2] + [other]
     barrier = pltpu.get_barrier_semaphore()
     for peer in peers:
         pl.semaphore_signal(barrier, inc=1, device_id=peer, device_id_type=MESH)
+    for there, peer in zip(has, (ahead, behind)):
+
+        @pl.when(there)
+        def greet(peer=peer):
+            pl.semaphore_signal(barrier, inc=1, device_id=peer, device_id_type=MESH)
+
     loads = [pltpu.make_async_copy(plan_in, plan_ref, plan_sem)] + [
         pltpu.make_async_copy(
             x_ref.at[:, pl.ds(s * BLK, BLK)], first.at[s], in_sem.at[s]
@@ -231,7 +234,7 @@
 
     shape = (8, LANES)
     reverse = LANES - 1 - lane_of((local_rows, LANES))
-    pl.semaphore_wait(barrier, len(peers))
+    pl.semaphore_wait(barrier, len(peers) + 2 - (index == 0) - (index == n_pairs - 1))
 
     def here(level, to):
         for peer in to:
@@ -308,15 +311,36 @@
         wide = [spread(line) for line in lines]
         return apply_steps(top, bottom, wide[:STEPS], wide[STEPS:])
 
+    def exchange(pairs_of_refs, send_sem, recv_sem):
+        for way, to in enumerate((ahead, behind)):
+
+            @pl.when(has[way])
+            def start(way=way, to=to):
+                for src, dst, which_core in pairs_of_refs(way):
+                    device_to = (z * 2 + which_core, to[1])
+                    remote(src, dst, send_sem.at[way], recv_sem.at[way], device_to).start()
+
+        def wait(ref, received):
+            for way in range(2):
+
+                @pl.when(sides_here[way] if received else has[way])
+                def one(way=way):
+                    copy = wait_all(ref.at[way], send_sem.at[way], recv_sem.at[way])
+                    if received:
+                        copy.wait_recv()
+                    else:
+                        copy.wait_send()
+
+        return wait
+
     for way, to in enumerate((ahead, behind)):
         sent[way] = first[slots_taken(0, to[1])]
-        remote(sent.at[way], came.at[way], block_out, block_in, to).start()
-    blocks = wait_all(came, block_out, block_in)
+    blocks = exchange(lambda way: [(sent.at[way], came.at[way], core)], block_out, block_in)
     known(0)
     here(1, line[2:])
     known(1)
     here(2, line[2:])
-    blocks.wait_recv()
+    blocks(came, True)
     band_sums(0, first, came)
     near_copies = send_near(0)
 
@@ -324,30 +348,30 @@
         from_second = slots_taken(1, to[1]) >= 2
         for side in range(2):
             cross[way, side] = jnp.where(from_second, sides[1, side], sides[0, side])
-        remote(cross.at[way], crossed.at[way], cross_out, cross_in, to).start()
-    columns = wait_all(crossed, cross_out, cross_in)
-    blocks.wait_send()
+    columns = exchange(lambda way: [(cross.at[way], crossed.at[way], core)], cross_out, cross_in)
+    blocks(came, False)
 
     total, far_copies = sum_rows(0, near_copies)
     cosines, sines = angles_of(total, entries.at[0])
     for k in range(STEPS):
         turns[core, k : k + 1] = cosines[k]
         turns[core, STEPS + k : STEPS + k + 1] = sines[k]
-    for way, to in both_cores:
-        remote(turns.at[core], far_turns.at[way, core], turn_out.at[0], turn_in.at[0], to).start()
-    far_angles = wait_all(far_turns, turn_out.at[0], turn_in.at[0])
+    far_angles = exchange(
+        lambda way: [(turns.at[core], far_turns.at[way, core], which) for which in (core, 1 - core)],
+        far_turn_out, far_turn_in,
+    )
     remote(turns.at[core], turns.at[core], turn_out.at[1], turn_in.at[1], other).start()
     angles_here = wait_all(turns.at[1 - core], turn_out.at[1], turn_in.at[1])
     far_copies.wait_send()
-    columns.wait_send()
+    columns(crossed, False)
     angles_here.wait_recv()
     for pair in range(2):
         lines = [turns[pair, k : k + 1] for k in range(2 * STEPS)]
         left, right = turned(sides[pair, 0], sides[pair, 1], lines)
         second[2 * pair] = left
         second[2 * pair + 1] = right
-    columns.wait_recv()
-    far_angles.wait_recv()
+    columns(crossed, True)
+    far_angles(far_turns, True)
     for way in range(2):
         took = jnp.int32(0)
         for s in range(SLOTS):
@@ -362,7 +386,7 @@
 
     band_sums(1, second, third)
     near_copies = send_near(1)
-    far_angles.wait_send()
+    far_angles(far_turns, False)
     angles_here.wait_send()
     total, far_copies = sum_rows(1, near_copies)
     cosines, sines = angles_of(total, entries.at[1])
@@ -413,14 +437,16 @@
             dma(()),
             pltpu.SemaphoreType.REGULAR((3,)),
             dma((SLOTS,)),
-            dma(()),
-            dma(()),
-            dma(()),
-            dma(()),
+            dma((2,)),
+            dma((2,)),
+            dma((2,)),
+            dma((2,)),
             dma((ROUNDS,)),
             dma((ROUNDS,)),
             dma((ROUNDS,)),
             dma((ROUNDS,)),
+            dma((2,)),
+            dma((2,)),
             dma((3,)),
             dma((3,)),
         ],

time: 48.4 us -> 44.1 us (0.911)
  the two profiles are of different devices: /device:TPU:1 before, /device:TPU:25 now
where the time goes in v5:
time: 44.1 us; the launch traced here: 43.9 us
  Pallas kernels  43.2 us (98%)
  local copies, waits for them, and re-layouts  0.71 us (2%)
    pallas_call x1, Pallas kernels, on_device(): pl.pallas_call(functools.partial(kernel, n_rows, n_pairs), out_shape=pltp...  43.2 us

profile of v5, /device:TPU:25, one launch (start us, length us, event | category | flops | bytes accessed | tf_op | source)
XLA Modules:
  0.0 43.9 jit_solution(11724309744278596922)
XLA Ops:
  0.0 43.2 %shard_map.28 = f32[128,512]{1,0:T(8,128)S(1)} custom-call(s32[2,64]{1,0:T(2,128)} %plan_in.1, f32[128,512]{1,0:T(8,128)} %x_ref.1), custom_call_target="tpu_custom_call" | custom-call | tf_op jit(solution)/shard_map/pallas_call | solution.py:412
  43.2 0.7 %copy.4 = f32[128,512]{1,0:T(8,128)} copy(f32[128,512]{1,0:T(8,128)S(1)} %shard_map.28) | data formatting | bytes 524288

commit v6 on v5

--- a/solution.py
+++ b/solution.py
@@ -384,6 +384,10 @@
         left, right = turned(crossed[way, 0], crossed[way, 1], lines)
         third[way] = jnp.where((took == 1) | (took == 3), right, left)
 
+    def place(pair, left, right):
+        o_ref[:, pl.ds(pl.multiple_of(2 * pair * BLK, BLK), BLK)] = left
+        o_ref[:, pl.ds(pl.multiple_of((2 * pair + 1) * BLK, BLK), BLK)] = right
+
     band_sums(1, second, third)
     near_copies = send_near(1)
     far_angles(far_turns, False)
@@ -396,13 +400,12 @@
     remote(last_turns.at[core], last_turns.at[core], turn_out.at[2], turn_in.at[2], other).start()
     angles_here = wait_all(last_turns.at[1 - core], turn_out.at[2], turn_in.at[2])
     far_copies.wait_send()
+    left, right = turned(sides[core, 0], sides[core, 1], cosines + sines)
+    place(core, left, right)
     angles_here.wait_recv()
-    for pair in range(2):
-        lines = [last_turns[pair, k : k + 1] for k in range(2 * STEPS)]
-        left, right = turned(sides[pair, 0], sides[pair, 1], lines)
-        o_ref[:, 2 * pair * BLK : (2 * pair + 1) * BLK] = left
-        o_ref[:, (2 * pair + 1) * BLK : (2 * pair + 2) * BLK] = right
-
+    lines = [last_turns[1 - core, k : k + 1] for k in range(2 * STEPS)]
+    left, right = turned(sides[1 - core, 0], sides[1 - core, 1], lines)
+    place(1 - core, left, right)
     angles_here.wait_send()
 
 

time: 44.1 us -> 43.8 us (level)
  no operation moved by 1% of the time
where the time goes in v6:
time: 43.8 us; the launch traced here: 43.6 us
  Pallas kernels  42.9 us (98%)
  local copies, waits for them, and re-layouts  0.71 us (2%)
    pallas_call x1, Pallas kernels, on_device(): pl.pallas_call(functools.partial(kernel, n_rows, n_pairs), out_shape=pltp...  42.9 us

profile of v6, /device:TPU:25, one launch (start us, length us, event | category | flops | bytes accessed | tf_op | source)
XLA Modules:
  0.0 43.6 jit_solution(15261351287324069756)
XLA Ops:
  0.0 42.9 %shard_map.28 = f32[128,512]{1,0:T(8,128)S(1)} custom-call(s32[2,64]{1,0:T(2,128)} %plan_in.1, f32[128,512]{1,0:T(8,128)} %x_ref.1), custom_call_target="tpu_custom_call" | custom-call | tf_op jit(solution)/shard_map/pallas_call | solution.py:415
  42.9 0.7 %copy.4 = f32[128,512]{1,0:T(8,128)} copy(f32[128,512]{1,0:T(8,128)S(1)} %shard_map.28) | data formatting | bytes 524288

commit v7 on v6

--- a/solution.py
+++ b/solution.py
@@ -264,15 +264,18 @@
             sides[pair, 1] = bottom
             for k in range(16):
                 bands[rnd, pair, k : k + 1] = jnp.sum(fold(terms[k]), axis=0, keepdims=True)
+            for which in (3, 2, 1):
+                remote(
+                    bands.at[rnd, pair], parts.at[rnd, which * 2 + (core + pair) % 2],
+                    part_out.at[rnd], part_in.at[rnd], device(partner[which], pair),
+                ).start()
 
     def wait_all(refs, send_sem, recv_sem):
         return remote(refs, refs, send_sem, recv_sem, other)
 
     def send_near(rnd):
-        for slot, there, to in near:
-            remote(
-                bands.at[rnd, there], parts.at[rnd, slot], part_out.at[rnd], part_in.at[rnd], to
-            ).start()
+        slot, there, to = near[-1]
+        remote(bands.at[rnd, there], parts.at[rnd, slot], part_out.at[rnd], part_in.at[rnd], to).start()
         parts[rnd, 0] = bands[rnd, core]
         return wait_all(parts.at[rnd, pl.ds(1, len(near))], part_out.at[rnd], part_in.at[rnd])
 

time: 43.8 us -> 43.2 us (0.986)
  the two profiles are of different devices: /device:TPU:25 before, /device:TPU:1 now
where the time goes in v7:
time: 43.2 us; the launch traced here: 42.4 us
  Pallas kernels  41.7 us (97%)
  local copies, waits for them, and re-layouts  0.71 us (2%)
    pallas_call x1, Pallas kernels, on_device(): pl.pallas_call(functools.partial(kernel, n_rows, n_pairs), out_shape=pltp...  41.7 us

profile of v7, /device:TPU:1, one launch (start us, length us, event | category | flops | bytes accessed | tf_op | source)
XLA Modules:
  0.0 42.4 jit_solution(8216345001925467)
XLA Ops:
  0.0 41.7 %shard_map.28 = f32[128,512]{1,0:T(8,128)S(1)} custom-call(s32[2,64]{1,0:T(2,128)} %plan_in.1, f32[128,512]{1,0:T(8,128)} %x_ref.1), custom_call_target="tpu_custom_call" | custom-call | tf_op jit(solution)/shard_map/pallas_call | solution.py:418
  41.7 0.7 %copy.4 = f32[128,512]{1,0:T(8,128)} copy(f32[128,512]{1,0:T(8,128)S(1)} %shard_map.28) | data formatting | bytes 524288
